TPU v7x, 256 devices: a whole 4x4x8 slice. The times are simulated.
256 devices in a mesh: tp: 4 (over x), ep: 64 (over z, y, core).
Axes of the slice: x: 4, y: 4, z: 8, core: 2. Of those that a mesh axis runs over, the one named last changes fastest.
Arguments:
- tokens: bfloat16 [32768, 2048], P(('tp', 'ep')), may hold values from -6 to 6
- expert_ids: int32 [32768, 2], P(('tp', 'ep')), may hold values from 0 to 255, all different within a row; in each aligned block of 128 rows (0 to 127, 128 to 255, ...) at most 2 rows name the same one
- gate_weights: float32 [32768, 2], P(('tp', 'ep')), may hold values from 0.1 to 1
- grad_out: bfloat16 [32768, 2048], P(('tp', 'ep')), may hold values from -6 to 6
- expert_gate: bfloat16 [256, 2048, 512], P(('tp', 'ep')), may hold values from -0.125 to 0.125
- expert_up: bfloat16 [256, 2048, 512], P(('tp', 'ep')), may hold values from -0.125 to 0.125
- expert_down: bfloat16 [256, 512, 2048], P(('tp', 'ep')), may hold values from -0.25 to 0.25
- shared_gate: bfloat16 [2048, 512], P(None, 'tp'), may hold values from -0.125 to 0.125
- shared_up: bfloat16 [2048, 512], P(None, 'tp'), may hold values from -0.125 to 0.125
- shared_down: bfloat16 [512, 2048], P('tp'), may hold values from -0.25 to 0.25
- shared_switch: bfloat16 [2048], replicated, may hold values from -0.29882812 to 0.29882812
Outputs:
- mixed: bfloat16 [32768, 2048], P(('tp', 'ep'))
- grad_tokens: bfloat16 [32768, 2048], P(('tp', 'ep'))
- gate_grad: float32 [32768, 2], P(('tp', 'ep'))
Inputs may be any that keep to these rules, and one draw needn't show every extreme that they name: `expert_ids`: each row names 2 different experts; among the rows of one device no expert is named more than 2 times, a bound that some block reaches.
All inputs are finite; a program needn't handle non-finite values.
Results may differ from a plain program's by a relative error of at most 0.019.
Values may be sent and summed in bfloat16 or wider, within the bound.
No kernel may reach another device: no remote copies, remote signals or barrier semaphores. Data moves between devices by JAX's collectives and lax.ppermute only.
A program may use at most 128 MiB of HBM per device.

v0:
```python
import jax
import jax.numpy as jnp
from jax import lax
from jax.sharding import PartitionSpec as P


def silu_grad(argument):
    gate_sig = jax.nn.sigmoid(argument)
    return gate_sig * (1.0 + argument * (1.0 - gate_sig))


def expert_slots(expert_ids, experts, capacity):
    chosen = expert_ids.reshape(-1)
    onehot = (chosen[:, None] == jnp.arange(experts, dtype=jnp.int32)[None, :]).astype(jnp.int32)
    before = jnp.cumsum(onehot, axis=0) - onehot
    position = jnp.sum(before * onehot, axis=1)
    return chosen * capacity + position


def expert_forward(slot_rows, weighting, expert_gate, expert_up, expert_down):
    pre_gate = jnp.einsum(
        "sjcd,jdf->sjcf", slot_rows, expert_gate, preferred_element_type=jnp.float32
    )
    pre_up = jnp.einsum("sjcd,jdf->sjcf", slot_rows, expert_up, preferred_element_type=jnp.float32)
    hidden = (jax.nn.silu(pre_gate) * pre_up).astype(jnp.bfloat16)
    output = jnp.einsum("sjcf,jfd->sjcd", hidden, expert_down, preferred_element_type=jnp.float32)
    routed = (weighting[..., None] * output).astype(jnp.bfloat16)
    return (pre_gate, pre_up, output, routed)


def expert_backward(
    cot_rows, weighting, pre_gate, pre_up, output, expert_gate, expert_up, expert_down
):
    cotangent = cot_rows.astype(jnp.float32)
    slot_grad = jnp.sum(cotangent * output, axis=3)
    scaled = (weighting[..., None] * cotangent).astype(jnp.bfloat16)
    hidden_grad = jnp.einsum(
        "sjcd,jfd->sjcf", scaled, expert_down, preferred_element_type=jnp.float32
    )
    gate_part = (hidden_grad * pre_up * silu_grad(pre_gate)).astype(jnp.bfloat16)
    up_part = (hidden_grad * jax.nn.silu(pre_gate)).astype(jnp.bfloat16)
    input_grad = (
        jnp.einsum("sjcf,jdf->sjcd", gate_part, expert_gate, preferred_element_type=jnp.float32)
        + jnp.einsum("sjcf,jdf->sjcd", up_part, expert_up, preferred_element_type=jnp.float32)
    ).astype(jnp.bfloat16)
    return (input_grad, slot_grad)


def local(
    tokens,
    expert_ids,
    gate_weights,
    grad_out,
    expert_gate,
    expert_up,
    expert_down,
    shared_gate,
    shared_up,
    shared_down,
    shared_switch,
):
    tp_count = lax.axis_size("tp")
    ep_count = lax.axis_size("ep")
    held_experts = expert_gate.shape[0]
    experts = held_experts * tp_count * ep_count
    tok_rows = tokens.shape[0]
    model_width = tokens.shape[1]
    routes_each = expert_ids.shape[1]
    capacity = max(2, 2 * tok_rows * routes_each // experts)
    slot_count = experts * capacity
    layout = (tp_count, ep_count, held_experts * capacity)
    sources = tp_count * ep_count
    slot_shape = (sources, held_experts, capacity, model_width)
    slot_index = expert_slots(expert_ids, experts, capacity)
    send_rows = (
        jnp.zeros((slot_count, model_width), jnp.bfloat16)
        .at[slot_index]
        .set(jnp.repeat(tokens, routes_each, axis=0))
    )
    send_gates = jnp.zeros((slot_count,), jnp.float32).at[slot_index].set(gate_weights.reshape(-1))
    send_cot = (
        jnp.zeros((slot_count, model_width), jnp.bfloat16)
        .at[slot_index]
        .set(jnp.repeat(grad_out, routes_each, axis=0))
    )
    arrived, arrived_gates = (
        lax.all_to_all(
            lax.all_to_all(
                send_rows.reshape(layout + (model_width,)),
                "tp",
                split_axis=0,
                concat_axis=0,
                tiled=True,
            ),
            "ep",
            split_axis=1,
            concat_axis=1,
            tiled=True,
        ),
        lax.all_to_all(
            lax.all_to_all(
                send_gates.reshape(layout).astype(jnp.bfloat16),
                "tp",
                split_axis=0,
                concat_axis=0,
                tiled=True,
            ),
            "ep",
            split_axis=1,
            concat_axis=1,
            tiled=True,
        ).astype(jnp.float32),
    )
    weighting = arrived_gates.reshape(sources, held_experts, capacity)
    pre_gate, pre_up, output, routed = expert_forward(
        arrived.reshape(slot_shape), weighting, expert_gate, expert_up, expert_down
    )
    routed_back = lax.all_to_all(
        lax.all_to_all(
            routed.reshape(layout + (model_width,)), "tp", split_axis=0, concat_axis=0, tiled=True
        ),
        "ep",
        split_axis=1,
        concat_axis=1,
        tiled=True,
    )
    arrived_cot = lax.all_to_all(
        lax.all_to_all(
            send_cot.reshape(layout + (model_width,)), "tp", split_axis=0, concat_axis=0, tiled=True
        ),
        "ep",
        split_axis=1,
        concat_axis=1,
        tiled=True,
    )
    input_grad, slot_grad = expert_backward(
        arrived_cot.reshape(slot_shape),
        weighting,
        pre_gate,
        pre_up,
        output,
        expert_gate,
        expert_up,
        expert_down,
    )
    grad_back, gate_back = (
        lax.all_to_all(
            lax.all_to_all(
                input_grad.reshape(layout + (model_width,)),
                "tp",
                split_axis=0,
                concat_axis=0,
                tiled=True,
            ),
            "ep",
            split_axis=1,
            concat_axis=1,
            tiled=True,
        ),
        lax.all_to_all(
            lax.all_to_all(
                slot_grad.reshape(layout).astype(jnp.bfloat16),
                "tp",
                split_axis=0,
                concat_axis=0,
                tiled=True,
            ),
            "ep",
            split_axis=1,
            concat_axis=1,
            tiled=True,
        ).astype(jnp.float32),
    )
    routed_sum = (
        routed_back.reshape(slot_count, model_width)[slot_index]
        .astype(jnp.float32)
        .reshape(tok_rows, routes_each, model_width)
        .sum(axis=1)
    )
    routed_grad = (
        grad_back.reshape(slot_count, model_width)[slot_index]
        .astype(jnp.float32)
        .reshape(tok_rows, routes_each, model_width)
        .sum(axis=1)
    )
    gate_grad = gate_back.reshape(slot_count)[slot_index].reshape(tok_rows, routes_each)
    switch_logit = jnp.dot(tokens, shared_switch, preferred_element_type=jnp.float32)
    switch = jax.nn.sigmoid(switch_logit)
    shared_cot = (switch[:, None] * grad_out.astype(jnp.float32)).astype(jnp.bfloat16)
    gathered = lax.all_gather(tokens, "tp", axis=0, tiled=True)
    shared_pre_gate = jnp.dot(gathered, shared_gate, preferred_element_type=jnp.float32)
    shared_pre_up = jnp.dot(gathered, shared_up, preferred_element_type=jnp.float32)
    shared_hidden = (jax.nn.silu(shared_pre_gate) * shared_pre_up).astype(jnp.bfloat16)
    shared = lax.psum_scatter(
        jnp.dot(shared_hidden, shared_down, preferred_element_type=jnp.float32).astype(
            jnp.bfloat16
        ),
        "tp",
        scatter_dimension=0,
        tiled=True,
    ).astype(jnp.float32)
    cot_gathered = lax.all_gather(shared_cot, "tp", axis=0, tiled=True)
    shared_hidden_grad = jnp.einsum(
        "td,fd->tf", cot_gathered, shared_down, preferred_element_type=jnp.float32
    )
    shared_gate_part = (shared_hidden_grad * shared_pre_up * silu_grad(shared_pre_gate)).astype(
        jnp.bfloat16
    )
    shared_up_part = (shared_hidden_grad * jax.nn.silu(shared_pre_gate)).astype(jnp.bfloat16)
    shared_input_grad = lax.psum_scatter(
        (
            jnp.einsum(
                "tf,df->td", shared_gate_part, shared_gate, preferred_element_type=jnp.float32
            )
            + jnp.einsum("tf,df->td", shared_up_part, shared_up, preferred_element_type=jnp.float32)
        ).astype(jnp.bfloat16),
        "tp",
        scatter_dimension=0,
        tiled=True,
    ).astype(jnp.float32)
    mixed = (switch[:, None] * shared + routed_sum).astype(jnp.bfloat16)
    switch_grad = switch * (1.0 - switch) * jnp.sum(grad_out.astype(jnp.float32) * shared, axis=1)
    grad_tokens = (
        shared_input_grad
        + routed_grad
        + switch_grad[:, None] * shared_switch.astype(jnp.float32)[None, :]
    ).astype(jnp.bfloat16)
    return (mixed, grad_tokens, gate_grad)


def solution(mesh):
    placed = (
        P(("tp", "ep"), None),
        P(("tp", "ep"), None),
        P(("tp", "ep"), None),
        P(("tp", "ep"), None),
        P(("tp", "ep"), None, None),
        P(("tp", "ep"), None, None),
        P(("tp", "ep"), None, None),
        P(None, "tp"),
        P(None, "tp"),
        P("tp", None),
        P(),
    )
    return jax.shard_map(
        local,
        mesh=mesh,
        in_specs=placed,
        out_specs=(P(("tp", "ep"), None), P(("tp", "ep"), None), P(("tp", "ep"), None)),
        check_vma=False,
    )
```

profile of v0, /device:TPU:8, one launch (start us, length us, event | category | flops | bytes accessed | tf_op | source)
XLA Modules:
  0.0 523.2 jit_solution(11906621634185771568)
XLA Ops:
  12.6 9.3 %all_to_all.60 = bf16[4,64,2]{1,2,0:T(2,128)(2,1)S(1)} all-to-all(bf16[4,64,2]{1,2,0:T(2,128)(2,1)S(1)} %copy.82), channel_id=1, replica_groups=mesh['tp'=4,'ep'=64] {'tp'}, dimensions={0} | all-to-all | bytes 2048 | tf_op jit(solution)/shard_map/all_to_all | solution.py:101
  22.7 12.1 %all-to-all-start.1 = ((bf16[4,64,2]{0,2,1:T(2,128)(2,1)}), bf16[4,64,2]{0,2,1:T(2,128)(2,1)S(1)}, u32[]{:S(2)}, u32[]{:S(2)}) async-start(bf16[4,64,2]{0,2,1:T(2,128)(2,1)} %copy.83), calls=%async_computation.2 | async-start | bytes 65536 | tf_op jit(solution)/shard_map/all_to_all | solution.py:100
  62.3 15.2 %all-to-all-done.2 = bf16[4,64,2,2048]{3,2,1,0:T(2,128)(2,1)} async-done(((bf16[4,64,2,2048]{3,2,1,0:T(2,128)(2,1)}), bf16[4,64,2,2048]{3,2,1,0:T(2,128)(2,1)}, u32[]{:S(2)}, u32[]{:S(2)}) %all-to-all-start.2) | async-done | bytes 2097184 | tf_op jit(solution)/shard_map/all_to_all | solution.py:88
  77.5 4.7 all-to-all-start.6
  82.2 5.5 %copy.85 = bf16[4,64,2,2048]{3,2,0,1:T(2,128)(2,1)} copy(bf16[4,64,2,2048]{3,2,1,0:T(2,128)(2,1)} %all-to-all-done.2) | data formatting | bytes 4194304 | tf_op jit(solution)/shard_map/all_to_all | solution.py:88
  87.6 20.7 %all-to-all-done.6 = bf16[4,64,2,2048]{3,2,1,0:T(2,128)(2,1)} async-done(((bf16[4,64,2,2048]{3,2,1,0:T(2,128)(2,1)}), bf16[4,64,2,2048]{3,2,1,0:T(2,128)(2,1)}, u32[]{:S(2)}, u32[]{:S(2)}) %all-to-all-start.6) | async-done | bytes 2097184 | tf_op jit(solution)/shard_map/all_to_all | solution.py:128
  108.3 10.5 %all-to-all-start.3 = ((bf16[4,64,2,2048]{3,2,0,1:T(2,128)(2,1)}), bf16[4,64,2,2048]{3,2,0,1:T(2,128)(2,1)}, u32[]{:S(2)}, u32[]{:S(2)}) async-start(bf16[4,64,2,2048]{3,2,0,1:T(2,128)(2,1)} %copy.85), calls=%async_computation.4 | async-start | bytes 4194304 | tf_op jit(solution)/shard_map/all_to_all | solution.py:87
  118.8 5.4 %copy.90 = bf16[4,64,2,2048]{3,2,0,1:T(2,128)(2,1)} copy(bf16[4,64,2,2048]{3,2,1,0:T(2,128)(2,1)} %all-to-all-done.6) | data formatting | bytes 4194304 | tf_op jit(solution)/shard_map/all_to_all | solution.py:128
  124.2 45.8 %all-to-all-done.3 = bf16[4,64,2,2048]{3,2,0,1:T(2,128)(2,1)} async-done(((bf16[4,64,2,2048]{3,2,0,1:T(2,128)(2,1)}), bf16[4,64,2,2048]{3,2,0,1:T(2,128)(2,1)}, u32[]{:S(2)}, u32[]{:S(2)}) %all-to-all-start.3) | async-done | bytes 2097184 | tf_op jit(solution)/shard_map/all_to_all | solution.py:87
  170.0 5.6 %all-to-all-start.7 = ((bf16[4,64,2,2048]{3,2,0,1:T(2,128)(2,1)}), bf16[4,64,2,2048]{3,2,0,1:T(2,128)(2,1)}, u32[]{:S(2)}, u32[]{:S(2)}) async-start(bf16[4,64,2,2048]{3,2,0,1:T(2,128)(2,1)} %copy.90), calls=%async_computation.9 | async-start | bytes 4194304 | tf_op jit(solution)/shard_map/all_to_all | solution.py:127
  183.3 43.5 %all-to-all-done.7 = bf16[4,64,2,2048]{3,2,0,1:T(2,128)(2,1)} async-done(((bf16[4,64,2,2048]{3,2,0,1:T(2,128)(2,1)}), bf16[4,64,2,2048]{3,2,0,1:T(2,128)(2,1)}, u32[]{:S(2)}, u32[]{:S(2)}) %all-to-all-start.7) | async-done | bytes 2097184 | tf_op jit(solution)/shard_map/all_to_all | solution.py:127
  232.7 4.6 all-to-all-start.4
  243.8 28.6 %all-to-all-done.4 = bf16[4,64,2,2048]{3,1,2,0:T(8,128)(2,1)} async-done(((bf16[4,64,2,2048]{3,1,2,0:T(8,128)(2,1)}), bf16[4,64,2,2048]{3,1,2,0:T(8,128)(2,1)}, u32[]{:S(2)}, u32[]{:S(2)}) %all-to-all-start.4) | async-done | bytes 2097184 | tf_op jit(solution)/shard_map/all_to_all | solution.py:119
  272.4 4.6 copy.88
  277.0 6.2 %all-to-all-start.5 = ((bf16[4,64,2,2048]{3,0,2,1:T(4,128)(2,1)}), bf16[4,64,2,2048]{3,0,2,1:T(4,128)(2,1)}, u32[]{:S(2)}, u32[]{:S(2)}) async-start(bf16[4,64,2,2048]{3,0,2,1:T(4,128)(2,1)} %copy.88), calls=%async_computation.6 | async-start | bytes 4194304 | tf_op jit(solution)/shard_map/all_to_all | solution.py:118
  284.2 50.2 %all-to-all-done.5 = bf16[4,64,2,2048]{3,0,2,1:T(4,128)(2,1)} async-done(((bf16[4,64,2,2048]{3,0,2,1:T(4,128)(2,1)}), bf16[4,64,2,2048]{3,0,2,1:T(4,128)(2,1)}, u32[]{:S(2)}, u32[]{:S(2)}) %all-to-all-start.5) | async-done | bytes 2097184 | tf_op jit(solution)/shard_map/all_to_all | solution.py:118
  337.6 5.1 copy.89
  369.7 4.7 all-to-all-start.8
  375.2 37.7 %all-to-all-done.8 = bf16[4,64,2,2048]{3,1,2,0:T(8,128)(2,1)} async-done(((bf16[4,64,2,2048]{3,1,2,0:T(8,128)(2,1)}), bf16[4,64,2,2048]{3,1,2,0:T(8,128)(2,1)}, u32[]{:S(2)}, u32[]{:S(2)}) %all-to-all-start.8) | async-done | bytes 2097184 | tf_op jit(solution)/shard_map/all_to_all | solution.py:148
  412.9 9.8 %all-to-all-start.11 = ((bf16[4,64,2]{0,2,1:T(2,128)(2,1)}), bf16[4,64,2]{0,2,1:T(2,128)(2,1)S(1)}, u32[]{:S(2)}, u32[]{:S(2)}) async-start(bf16[4,64,2]{0,2,1:T(2,128)(2,1)} %copy.96), calls=%async_computation.13 | async-start | bytes 65536 | tf_op jit(solution)/shard_map/all_to_all | solution.py:160
  422.7 4.6 copy.93
  432.5 10.6 %all-to-all-start.9 = ((bf16[4,64,2,2048]{3,0,2,1:T(4,128)(2,1)}), bf16[4,64,2,2048]{3,0,2,1:T(4,128)(2,1)}, u32[]{:S(2)}, u32[]{:S(2)}) async-start(bf16[4,64,2,2048]{3,0,2,1:T(4,128)(2,1)} %copy.93), calls=%async_computation.11 | async-start | bytes 4194304 | tf_op jit(solution)/shard_map/all_to_all | solution.py:147
  450.8 43.5 %all-to-all-done.9 = bf16[4,64,2,2048]{3,0,2,1:T(4,128)(2,1)} async-done(((bf16[4,64,2,2048]{3,0,2,1:T(4,128)(2,1)}), bf16[4,64,2,2048]{3,0,2,1:T(4,128)(2,1)}, u32[]{:S(2)}, u32[]{:S(2)}) %all-to-all-start.9) | async-done | bytes 2097184 | tf_op jit(solution)/shard_map/all_to_all | solution.py:147
  494.3 5.1 copy.94
  (134 shorter events, 114.8 us)
Async XLA Ops:
  7.2 222.5 %copy-start = (bf16[1,512,2048]{2,1,0:T(8,128)(2,1)S(1)}, bf16[1,512,2048]{2,1,0:T(8,128)(2,1)}, u32[]{:S(2)}) copy-start(bf16[1,512,2048]{2,1,0:T(8,128)(2,1)} %param.17) | copy-start | bytes 6291460
  7.2 27.6 %copy-start.2 = (bf16[128,2048]{1,0:T(8,128)(2,1)S(1)}, bf16[128,2048]{1,0:T(8,128)(2,1)}, u32[]{:S(2)}) copy-start(bf16[128,2048]{1,0:T(8,128)(2,1)} %param.11) | copy-start | bytes 1572868
  22.7 23.3 %all-to-all-start.1 = ((bf16[4,64,2]{0,2,1:T(2,128)(2,1)}), bf16[4,64,2]{0,2,1:T(2,128)(2,1)S(1)}, u32[]{:S(2)}, u32[]{:S(2)}) async-start(bf16[4,64,2]{0,2,1:T(2,128)(2,1)} %copy.83), calls=%async_computation.2 | async-start | bytes 65536 | tf_op jit(solution)/shard_map/all_to_all | solution.py:100
  46.0 31.5 %all-to-all-start.2 = ((bf16[4,64,2,2048]{3,2,1,0:T(2,128)(2,1)}), bf16[4,64,2,2048]{3,2,1,0:T(2,128)(2,1)}, u32[]{:S(2)}, u32[]{:S(2)}) async-start(bf16[4,64,2,2048]{3,2,1,0:T(2,128)(2,1)} %reshape.170), calls=%async_computation.3 | async-start | bytes 4194304 | tf_op jit(solution)/shard_map/all_to_all | solution.py:88
  77.5 30.8 %all-to-all-start.6 = ((bf16[4,64,2,2048]{3,2,1,0:T(2,128)(2,1)}), bf16[4,64,2,2048]{3,2,1,0:T(2,128)(2,1)}, u32[]{:S(2)}, u32[]{:S(2)}) async-start(bf16[4,64,2,2048]{3,2,1,0:T(2,128)(2,1)} %reshape.179), calls=%async_computation.8 | async-start | bytes 4194304 | tf_op jit(solution)/shard_map/all_to_all | solution.py:128
  108.3 61.7 %all-to-all-start.3 = ((bf16[4,64,2,2048]{3,2,0,1:T(2,128)(2,1)}), bf16[4,64,2,2048]{3,2,0,1:T(2,128)(2,1)}, u32[]{:S(2)}, u32[]{:S(2)}) async-start(bf16[4,64,2,2048]{3,2,0,1:T(2,128)(2,1)} %copy.85), calls=%async_computation.4 | async-start | bytes 4194304 | tf_op jit(solution)/shard_map/all_to_all | solution.py:87
  170.0 56.8 %all-to-all-start.7 = ((bf16[4,64,2,2048]{3,2,0,1:T(2,128)(2,1)}), bf16[4,64,2,2048]{3,2,0,1:T(2,128)(2,1)}, u32[]{:S(2)}, u32[]{:S(2)}) async-start(bf16[4,64,2,2048]{3,2,0,1:T(2,128)(2,1)} %copy.90), calls=%async_computation.9 | async-start | bytes 4194304 | tf_op jit(solution)/shard_map/all_to_all | solution.py:127
  175.6 62.2 %all-gather.3.cloned.1.call-start = ((), (), s32[]{:S(2)}) async-start(), calls=%async_computation.14 | async-start | bytes 2621440 | tf_op jit(solution)/shard_map/all_gather | solution.py:190
  181.0 48.7 %copy-start.14 = (f32[256,1,2,512]{3,0,2,1:T(8,128)}, f32[256,1,2,512]{3,0,2,1:T(8,128)S(1)}, u32[]{:S(2)}) copy-start(f32[256,1,2,512]{3,0,2,1:T(8,128)S(1)} %fusion.13) | copy-start | bytes 3145732
  232.7 5.1 copy-start.12
  232.7 39.7 %all-to-all-start.4 = ((bf16[4,64,2,2048]{3,1,2,0:T(8,128)(2,1)}), bf16[4,64,2,2048]{3,1,2,0:T(8,128)(2,1)}, u32[]{:S(2)}, u32[]{:S(2)}) async-start(bf16[4,64,2,2048]{3,1,2,0:T(8,128)(2,1)} %copy.87), calls=%async_computation.5 | async-start | bytes 4194304 | tf_op jit(solution)/shard_map/all_to_all | solution.py:119
  237.3 3.0 copy-start.6
  237.3 120.4 %reduce-scatter.3.cloned.1.call-start = ((), (), s32[]{:S(2)}) async-start(), calls=%async_computation.15 | async-start | bytes 2621440 | tf_op jit(solution)/shard_map/reduce_scatter | solution.py:194
  277.0 6.2 %copy-start.16 = (bf16[2048]{0:T(1024)(128)(2,1)S(1)}, bf16[2048]{0:T(1024)(128)(2,1)}, u32[]{:S(2)}) copy-start(bf16[2048]{0:T(1024)(128)(2,1)} %param.21) | copy-start | bytes 12292
  277.0 6.2 %copy-start.3 = (bf16[128,2048]{1,0:T(8,128)(2,1)S(1)}, bf16[128,2048]{1,0:T(8,128)(2,1)}, u32[]{:S(2)}) copy-start(bf16[128,2048]{1,0:T(8,128)(2,1)} %param.11) | copy-start | bytes 1572868
  277.0 57.3 %all-to-all-start.5 = ((bf16[4,64,2,2048]{3,0,2,1:T(4,128)(2,1)}), bf16[4,64,2,2048]{3,0,2,1:T(4,128)(2,1)}, u32[]{:S(2)}, u32[]{:S(2)}) async-start(bf16[4,64,2,2048]{3,0,2,1:T(4,128)(2,1)} %copy.88), calls=%async_computation.6 | async-start | bytes 4194304 | tf_op jit(solution)/shard_map/all_to_all | solution.py:118
  334.4 35.3 %all-to-all-start.10 = ((bf16[4,64,2]{1,2,0:T(2,128)(2,1)}), bf16[4,64,2]{1,2,0:T(2,128)(2,1)S(1)}, u32[]{:S(2)}, u32[]{:S(2)}) async-start(bf16[4,64,2]{1,2,0:T(2,128)(2,1)} %copy.95), calls=%async_computation.12 | async-start | bytes 4096 | tf_op jit(solution)/shard_map/all_to_all | solution.py:161
  337.5 89.8 %all-gather.5.cloned.1.call-start = ((), (), s32[]{:S(2)}) async-start(), calls=%async_computation.16 | async-start | bytes 2621440 | tf_op jit(solution)/shard_map/all_gather | solution.py:202
  369.7 43.2 %all-to-all-start.8 = ((bf16[4,64,2,2048]{3,1,2,0:T(8,128)(2,1)}), bf16[4,64,2,2048]{3,1,2,0:T(8,128)(2,1)}, u32[]{:S(2)}, u32[]{:S(2)}) async-start(bf16[4,64,2,2048]{3,1,2,0:T(8,128)(2,1)} %copy.92), calls=%async_computation.10 | async-start | bytes 4194304 | tf_op jit(solution)/shard_map/all_to_all | solution.py:148
  412.9 19.6 %all-to-all-start.11 = ((bf16[4,64,2]{0,2,1:T(2,128)(2,1)}), bf16[4,64,2]{0,2,1:T(2,128)(2,1)S(1)}, u32[]{:S(2)}, u32[]{:S(2)}) async-start(bf16[4,64,2]{0,2,1:T(2,128)(2,1)} %copy.96), calls=%async_computation.13 | async-start | bytes 65536 | tf_op jit(solution)/shard_map/all_to_all | solution.py:160
  422.7 4.7 copy-start.11
  432.5 10.9 %copy-start.7 = (bf16[2048,128]{1,0:T(8,128)(2,1)S(1)}, bf16[2048,128]{1,0:T(8,128)(2,1)}, u32[]{:S(2)}) copy-start(bf16[2048,128]{1,0:T(8,128)(2,1)} %param.19) | copy-start | bytes 1572868
  432.5 61.8 %all-to-all-start.9 = ((bf16[4,64,2,2048]{3,0,2,1:T(4,128)(2,1)}), bf16[4,64,2,2048]{3,0,2,1:T(4,128)(2,1)}, u32[]{:S(2)}, u32[]{:S(2)}) async-start(bf16[4,64,2,2048]{3,0,2,1:T(4,128)(2,1)} %copy.93), calls=%async_computation.11 | async-start | bytes 4194304 | tf_op jit(solution)/shard_map/all_to_all | solution.py:147
  443.1 71.1 %reduce-scatter.5.cloned.1.call-start = ((), (), s32[]{:S(2)}) async-start(), calls=%async_computation.17 | async-start | bytes 2621440 | tf_op jit(solution)/shard_map/reduce_scatter | solution.py:210
  (12 other events, 23.9 us)
Sparse Core Ops, SparseCore 0:
  178.3 32.5 all-gather.2
  243.9 36.4 reduce-scatter.2
  360.4 42.1 all-gather.4
  447.8 31.6 reduce-scatter.4
where the time goes:
time: 533 us; the launch traced here: 523 us
  waiting for transfers between devices  286 us (54%)
  local copies, waits for them, and re-layouts  92.2 us (17%)
  starting transfers between devices  77.2 us (14%)
  matrix products  23.8 us (4%)
  other arithmetic  19.9 us (4%)
  between operations  14.8 us (3%)
  blocking collectives  9.35 us (2%)
    all_to_all x1, waiting for transfers between devices, local(): lax.all_to_all(lax.all_to_all(routed.reshape(layout + (model_width,)), 't...  50.2 us
    all_to_all x1, waiting for transfers between devices, local(): lax.all_to_all(lax.all_to_all(send_rows.reshape(layout + (model_width,)),...  45.8 us
    all_to_all x1, waiting for transfers between devices, local(): lax.all_to_all(lax.all_to_all(send_cot.reshape(layout + (model_width,)),...  43.5 us
    all_to_all x1, waiting for transfers between devices, local(): lax.all_to_all(lax.all_to_all(input_grad.reshape(layout + (model_width,))...  43.5 us
    all_to_all x1, waiting for transfers between devices, local(): lax.all_to_all(input_grad.reshape(layout + (model_width,)), 'tp', split_a...  37.7 us
    all_to_all x1, waiting for transfers between devices, local(): lax.all_to_all(routed.reshape(layout + (model_width,)), 'tp', split_axis=...  28.6 us
    all_to_all x1, waiting for transfers between devices, local(): lax.all_to_all(send_cot.reshape(layout + (model_width,)), 'tp', split_axi...  20.7 us
    all_to_all x1, waiting for transfers between devices, local(): lax.all_to_all(send_rows.reshape(layout + (model_width,)), 'tp', split_ax...  15.2 us
  transfers between devices with their start and end apart: 15, of which 8 were waited for; matrix products, arithmetic and copies ran while one was open for 24% of the time, Pallas kernels for 0%

commit v1 on v0

--- a/solution.py
+++ b/solution.py
@@ -157,18 +157,26 @@
             concat_axis=1,
             tiled=True,
         ),
-        lax.all_to_all(
-            lax.all_to_all(
-                slot_grad.reshape(layout).astype(jnp.bfloat16),
-                "tp",
-                split_axis=0,
-                concat_axis=0,
-                tiled=True,
-            ),
-            "ep",
-            split_axis=1,
-            concat_axis=1,
-            tiled=True,
+        jnp.concatenate(
+            lax.all_to_all(
+                jnp.stack(
+                    jnp.split(
+                        lax.all_to_all(
+                            slot_grad.reshape(layout).astype(jnp.bfloat16),
+                            "tp",
+                            split_axis=0,
+                            concat_axis=0,
+                            tiled=True,
+                        ),
+                        lax.axis_size("ep"),
+                        axis=1,
+                    )
+                ),
+                "ep",
+                0,
+                0,
+            ),
+            axis=1,
         ).astype(jnp.float32),
     )
     routed_sum = (

time: 533 us -> 493 us (0.925)
  waiting for transfers between devices: 286 us -> 215 us
  local copies, waits for them, and re-layouts: 92.2 us -> 123 us
    all_to_all x1, waiting for transfers between devices: 37.7 us -> 0.71 us  [local(): lax.all_to_all(input_grad.reshape(layout + (model_width,)), 'tp', split_a...]
    unnamed x47 -> x106, local copies, waits for them, and re-layouts: 4.25 us -> 38 us
    all_to_all x1, waiting for transfers between devices: 28.6 us -> 4.74 us  [local(): lax.all_to_all(routed.reshape(layout + (model_width,)), 'tp', split_axis=...]
    all_to_all x1, waiting for transfers between devices: 50.2 us -> 38.6 us  [local(): lax.all_to_all(lax.all_to_all(routed.reshape(layout + (model_width,)), 't...]
    all_gather x1, waiting for transfers between devices: 0.01 us -> 8.21 us  [local(): cot_gathered = lax.all_gather(shared_cot, 'tp', axis=0, tiled=True)]
    split x0 -> x68, local copies, waits for them, and re-layouts: none -> 7.58 us  [local(): jnp.split(lax.all_to_all(slot_grad.reshape(layout).astype(jnp.bfloat16),...]
    all_to_all x1, waiting for transfers between devices: 43.5 us -> 37.7 us  [local(): lax.all_to_all(lax.all_to_all(send_cot.reshape(layout + (model_width,)),...]
  transfers between devices with their start and end apart: 15 -> 15, of which waited for: 8 -> 9; matrix products, arithmetic and copies ran while one was open for 24% -> 33% of each run, Pallas kernels for 0% -> 0%
where the time goes in v1:
time: 493 us; the launch traced here: 484 us
  waiting for transfers between devices  215 us (44%)
  local copies, waits for them, and re-layouts  123 us (25%)
  starting transfers between devices  75.2 us (15%)
  matrix products  28.6 us (6%)
  other arithmetic  18.5 us (4%)
  between operations  14.6 us (3%)
  blocking collectives  9.35 us (2%)
    all_to_all x1, waiting for transfers between devices, local(): lax.all_to_all(lax.all_to_all(send_rows.reshape(layout + (model_width,)),...  45 us
    all_to_all x1, waiting for transfers between devices, local(): lax.all_to_all(lax.all_to_all(input_grad.reshape(layout + (model_width,))...  43.3 us
    all_to_all x1, waiting for transfers between devices, local(): lax.all_to_all(lax.all_to_all(routed.reshape(layout + (model_width,)), 't...  38.6 us
    unnamed x106, local copies, waits for them, and re-layouts  38 us
    all_to_all x1, waiting for transfers between devices, local(): lax.all_to_all(lax.all_to_all(send_cot.reshape(layout + (model_width,)),...  37.7 us
    all_to_all x1, waiting for transfers between devices, local(): lax.all_to_all(send_cot.reshape(layout + (model_width,)), 'tp', split_axi...  20.7 us
    all_to_all x1, waiting for transfers between devices, local(): lax.all_to_all(send_rows.reshape(layout + (model_width,)), 'tp', split_ax...  15.2 us
    all_to_all x1, starting transfers between devices, local(): lax.all_to_all(lax.all_to_all(send_gates.reshape(layout).astype(jnp.bfloa...  12.1 us
  transfers between devices with their start and end apart: 15, of which 9 were waited for; matrix products, arithmetic and copies ran while one was open for 33% of the time, Pallas kernels for 0%

profile of v1, /device:TPU:8, one launch (start us, length us, event | category | flops | bytes accessed | tf_op | source)
XLA Modules:
  0.0 483.8 jit_solution(4202904145339863378)
XLA Ops:
  12.6 9.3 %all_to_all.60 = bf16[4,64,2]{1,2,0:T(2,128)(2,1)S(1)} all-to-all(bf16[4,64,2]{1,2,0:T(2,128)(2,1)S(1)} %copy.590), channel_id=1, replica_groups=mesh['tp'=4,'ep'=64] {'tp'}, dimensions={0} | all-to-all | bytes 2048 | tf_op jit(solution)/shard_map/all_to_all | solution.py:101
  22.7 12.1 %all-to-all-start.1 = ((bf16[4,64,2]{0,2,1:T(2,128)(2,1)}), bf16[4,64,2]{0,2,1:T(2,128)(2,1)S(1)}, u32[]{:S(2)}, u32[]{:S(2)}) async-start(bf16[4,64,2]{0,2,1:T(2,128)(2,1)} %copy.591), calls=%async_computation.2 | async-start | bytes 65536 | tf_op jit(solution)/shard_map/all_to_all | solution.py:100
  53.4 4.5 scatter_custom_fusion.2
  62.3 15.2 %all-to-all-done.2 = bf16[4,64,2,2048]{3,2,1,0:T(2,128)(2,1)} async-done(((bf16[4,64,2,2048]{3,2,1,0:T(2,128)(2,1)}), bf16[4,64,2,2048]{3,2,1,0:T(2,128)(2,1)}, u32[]{:S(2)}, u32[]{:S(2)}) %all-to-all-start.2) | async-done | bytes 2097184 | tf_op jit(solution)/shard_map/all_to_all | solution.py:88
  77.5 4.6 all-to-all-start.6
  82.1 5.5 %copy.593 = bf16[4,64,2,2048]{3,2,0,1:T(2,128)(2,1)} copy(bf16[4,64,2,2048]{3,2,1,0:T(2,128)(2,1)} %all-to-all-done.2) | data formatting | bytes 4194304 | tf_op jit(solution)/shard_map/all_to_all | solution.py:88
  87.6 20.7 %all-to-all-done.6 = bf16[4,64,2,2048]{3,2,1,0:T(2,128)(2,1)} async-done(((bf16[4,64,2,2048]{3,2,1,0:T(2,128)(2,1)}), bf16[4,64,2,2048]{3,2,1,0:T(2,128)(2,1)}, u32[]{:S(2)}, u32[]{:S(2)}) %all-to-all-start.6) | async-done | bytes 2097184 | tf_op jit(solution)/shard_map/all_to_all | solution.py:128
  108.3 10.5 %all-to-all-start.3 = ((bf16[4,64,2,2048]{3,2,0,1:T(2,128)(2,1)}), bf16[4,64,2,2048]{3,2,0,1:T(2,128)(2,1)}, u32[]{:S(2)}, u32[]{:S(2)}) async-start(bf16[4,64,2,2048]{3,2,0,1:T(2,128)(2,1)} %copy.593), calls=%async_computation.4 | async-start | bytes 4194304 | tf_op jit(solution)/shard_map/all_to_all | solution.py:87
  119.5 5.4 %copy.598 = bf16[4,64,2,2048]{3,2,0,1:T(2,128)(2,1)} copy(bf16[4,64,2,2048]{3,2,1,0:T(2,128)(2,1)} %all-to-all-done.6) | data formatting | bytes 4194304 | tf_op jit(solution)/shard_map/all_to_all | solution.py:128
  124.9 45.0 %all-to-all-done.3 = bf16[4,64,2,2048]{3,2,0,1:T(2,128)(2,1)} async-done(((bf16[4,64,2,2048]{3,2,0,1:T(2,128)(2,1)}), bf16[4,64,2,2048]{3,2,0,1:T(2,128)(2,1)}, u32[]{:S(2)}, u32[]{:S(2)}) %all-to-all-start.3) | async-done | bytes 2097184 | tf_op jit(solution)/shard_map/all_to_all | solution.py:87
  170.0 5.6 %all-to-all-start.7 = ((bf16[4,64,2,2048]{3,2,0,1:T(2,128)(2,1)}), bf16[4,64,2,2048]{3,2,0,1:T(2,128)(2,1)}, u32[]{:S(2)}, u32[]{:S(2)}) async-start(bf16[4,64,2,2048]{3,2,0,1:T(2,128)(2,1)} %copy.598), calls=%async_computation.9 | async-start | bytes 4194304 | tf_op jit(solution)/shard_map/all_to_all | solution.py:127
  189.0 37.7 %all-to-all-done.7 = bf16[4,64,2,2048]{3,2,0,1:T(2,128)(2,1)} async-done(((bf16[4,64,2,2048]{3,2,0,1:T(2,128)(2,1)}), bf16[4,64,2,2048]{3,2,0,1:T(2,128)(2,1)}, u32[]{:S(2)}, u32[]{:S(2)}) %all-to-all-start.7) | async-done | bytes 2097184 | tf_op jit(solution)/shard_map/all_to_all | solution.py:127
  250.2 4.7 all-to-all-start.4
  275.2 4.7 all-to-all-done.4
  280.0 4.6 copy.596
  284.6 6.8 %all-to-all-start.5 = ((bf16[4,64,2,2048]{3,0,2,1:T(4,128)(2,1)}), bf16[4,64,2,2048]{3,0,2,1:T(4,128)(2,1)S(1)}, u32[]{:S(2)}, u32[]{:S(2)}) async-start(bf16[4,64,2,2048]{3,0,2,1:T(4,128)(2,1)} %copy.596), calls=%async_computation.6 | async-start | bytes 4194304 | tf_op jit(solution)/shard_map/all_to_all | solution.py:118
  304.1 38.6 %all-to-all-done.5 = bf16[4,64,2,2048]{3,0,2,1:T(4,128)(2,1)S(1)} async-done(((bf16[4,64,2,2048]{3,0,2,1:T(4,128)(2,1)}), bf16[4,64,2,2048]{3,0,2,1:T(4,128)(2,1)S(1)}, u32[]{:S(2)}, u32[]{:S(2)}) %all-to-all-start.5) | async-done | bytes 2097184 | tf_op jit(solution)/shard_map/all_to_all | solution.py:118
  342.7 4.5 all-to-all-start.8
  372.4 6.8 %all-to-all-start.11 = ((bf16[64,4,1,2]{1,3,2,0:T(2,128)(2,1)}), bf16[64,4,1,2]{1,3,2,0:T(2,128)(2,1)S(1)}, u32[]{:S(2)}, u32[]{:S(2)}) async-start(bf16[64,4,1,2]{1,3,2,0:T(2,128)(2,1)} %constant_dynamic-update-slice_fusion), calls=%async_computation.13 | async-start | bytes 65536 | tf_op jit(solution)/shard_map/all_to_all | solution.py:161
  379.2 4.7 copy.601
  383.9 8.2 %all-gather.5.cloned.1.call-done = bf16[512,2048]{1,0:T(8,128)(2,1)} async-done(((bf16[128,2048]{1,0:T(8,128)(2,1)}), bf16[512,2048]{1,0:T(8,128)(2,1)}) %all-gather.5.cloned.1.call-update) | async-done | bytes 2097168 | tf_op jit(solution)/shard_map/all_gather | solution.py:210
  397.1 11.1 %all-to-all-start.9 = ((bf16[4,64,2,2048]{3,0,2,1:T(4,128)(2,1)}), bf16[4,64,2,2048]{3,0,2,1:T(4,128)(2,1)}, u32[]{:S(2)}, u32[]{:S(2)}) async-start(bf16[4,64,2,2048]{3,0,2,1:T(4,128)(2,1)} %copy.601), calls=%async_computation.11 | async-start | bytes 4194304 | tf_op jit(solution)/shard_map/all_to_all | solution.py:147
  416.0 43.3 %all-to-all-done.9 = bf16[4,64,2,2048]{3,0,2,1:T(4,128)(2,1)} async-done(((bf16[4,64,2,2048]{3,0,2,1:T(4,128)(2,1)}), bf16[4,64,2,2048]{3,0,2,1:T(4,128)(2,1)}, u32[]{:S(2)}, u32[]{:S(2)}) %all-to-all-start.9) | async-done | bytes 2097184 | tf_op jit(solution)/shard_map/all_to_all | solution.py:147
  459.3 5.1 %copy.602 = bf16[4,64,2,2048]{3,2,1,0:T(2,128)(2,1)} copy(bf16[4,64,2,2048]{3,0,2,1:T(4,128)(2,1)} %all-to-all-done.9) | data formatting | bytes 4194304 | tf_op jit(solution)/shard_map/all_to_all | solution.py:147
  (261 shorter events, 149.9 us)
Async XLA Ops:
  7.2 222.5 %copy-start = (bf16[1,512,2048]{2,1,0:T(8,128)(2,1)S(1)}, bf16[1,512,2048]{2,1,0:T(8,128)(2,1)}, u32[]{:S(2)}) copy-start(bf16[1,512,2048]{2,1,0:T(8,128)(2,1)} %param.17) | copy-start | bytes 6291460
  7.2 27.6 %copy-start.3 = (bf16[128,2048]{1,0:T(8,128)(2,1)S(1)}, bf16[128,2048]{1,0:T(8,128)(2,1)}, u32[]{:S(2)}) copy-start(bf16[128,2048]{1,0:T(8,128)(2,1)} %param.11) | copy-start | bytes 1572868
  22.7 23.4 %all-to-all-start.1 = ((bf16[4,64,2]{0,2,1:T(2,128)(2,1)}), bf16[4,64,2]{0,2,1:T(2,128)(2,1)S(1)}, u32[]{:S(2)}, u32[]{:S(2)}) async-start(bf16[4,64,2]{0,2,1:T(2,128)(2,1)} %copy.591), calls=%async_computation.2 | async-start | bytes 65536 | tf_op jit(solution)/shard_map/all_to_all | solution.py:100
  46.1 31.4 %all-to-all-start.2 = ((bf16[4,64,2,2048]{3,2,1,0:T(2,128)(2,1)}), bf16[4,64,2,2048]{3,2,1,0:T(2,128)(2,1)}, u32[]{:S(2)}, u32[]{:S(2)}) async-start(bf16[4,64,2,2048]{3,2,1,0:T(2,128)(2,1)} %reshape.170), calls=%async_computation.3 | async-start | bytes 4194304 | tf_op jit(solution)/shard_map/all_to_all | solution.py:88
  77.5 30.8 %all-to-all-start.6 = ((bf16[4,64,2,2048]{3,2,1,0:T(2,128)(2,1)}), bf16[4,64,2,2048]{3,2,1,0:T(2,128)(2,1)}, u32[]{:S(2)}, u32[]{:S(2)}) async-start(bf16[4,64,2,2048]{3,2,1,0:T(2,128)(2,1)} %reshape.179), calls=%async_computation.8 | async-start | bytes 4194304 | tf_op jit(solution)/shard_map/all_to_all | solution.py:128
  108.3 61.7 %all-to-all-start.3 = ((bf16[4,64,2,2048]{3,2,0,1:T(2,128)(2,1)}), bf16[4,64,2,2048]{3,2,0,1:T(2,128)(2,1)}, u32[]{:S(2)}, u32[]{:S(2)}) async-start(bf16[4,64,2,2048]{3,2,0,1:T(2,128)(2,1)} %copy.593), calls=%async_computation.4 | async-start | bytes 4194304 | tf_op jit(solution)/shard_map/all_to_all | solution.py:87
  118.8 57.4 %all-gather.3.cloned.1.call-start = ((), (), s32[]{:S(2)}) async-start(), calls=%async_computation.14 | async-start | bytes 2621440 | tf_op jit(solution)/shard_map/all_gather | solution.py:198
  124.9 50.7 %copy-start.16 = (bf16[2048]{0:T(1024)(128)(2,1)S(1)}, bf16[2048]{0:T(1024)(128)(2,1)}, u32[]{:S(2)}) copy-start(bf16[2048]{0:T(1024)(128)(2,1)} %param.21) | copy-start | bytes 12292
  124.9 50.7 %copy-start.4 = (bf16[128,2048]{1,0:T(8,128)(2,1)S(1)}, bf16[128,2048]{1,0:T(8,128)(2,1)}, u32[]{:S(2)}) copy-start(bf16[128,2048]{1,0:T(8,128)(2,1)} %param.11) | copy-start | bytes 1572868
  170.0 56.8 %all-to-all-start.7 = ((bf16[4,64,2,2048]{3,2,0,1:T(2,128)(2,1)}), bf16[4,64,2,2048]{3,2,0,1:T(2,128)(2,1)}, u32[]{:S(2)}, u32[]{:S(2)}) async-start(bf16[4,64,2,2048]{3,2,0,1:T(2,128)(2,1)} %copy.598), calls=%async_computation.9 | async-start | bytes 4194304 | tf_op jit(solution)/shard_map/all_to_all | solution.py:127
  175.6 183.8 %reduce-scatter.3.cloned.1.call-start = ((), (), s32[]{:S(2)}) async-start(), calls=%async_computation.15 | async-start | bytes 2621440 | tf_op jit(solution)/shard_map/reduce_scatter | solution.py:202
  238.3 11.9 %all-to-all-start.10 = ((bf16[4,64,2]{1,2,0:T(2,128)(2,1)}), bf16[4,64,2]{1,2,0:T(2,128)(2,1)S(1)}, u32[]{:S(2)}, u32[]{:S(2)}) async-start(bf16[4,64,2]{1,2,0:T(2,128)(2,1)} %copy.603), calls=%async_computation.12 | async-start | bytes 4096 | tf_op jit(solution)/shard_map/all_to_all | solution.py:164
  250.2 29.7 %all-to-all-start.4 = ((bf16[4,64,2,2048]{3,1,2,0:T(8,128)(2,1)}), bf16[4,64,2,2048]{3,1,2,0:T(8,128)(2,1)}, u32[]{:S(2)}, u32[]{:S(2)}) async-start(bf16[4,64,2,2048]{3,1,2,0:T(8,128)(2,1)} %copy.595), calls=%async_computation.5 | async-start | bytes 4194304 | tf_op jit(solution)/shard_map/all_to_all | solution.py:119
  284.6 58.1 %all-to-all-start.5 = ((bf16[4,64,2,2048]{3,0,2,1:T(4,128)(2,1)}), bf16[4,64,2,2048]{3,0,2,1:T(4,128)(2,1)S(1)}, u32[]{:S(2)}, u32[]{:S(2)}) async-start(bf16[4,64,2,2048]{3,0,2,1:T(4,128)(2,1)} %copy.596), calls=%async_computation.6 | async-start | bytes 4194304 | tf_op jit(solution)/shard_map/all_to_all | solution.py:118
  342.7 29.7 %all-to-all-start.8 = ((bf16[4,64,2,2048]{3,1,2,0:T(8,128)(2,1)}), bf16[4,64,2,2048]{3,1,2,0:T(8,128)(2,1)}, u32[]{:S(2)}, u32[]{:S(2)}) async-start(bf16[4,64,2,2048]{3,1,2,0:T(8,128)(2,1)} %copy.600), calls=%async_computation.10 | async-start | bytes 4194304 | tf_op jit(solution)/shard_map/all_to_all | solution.py:148
  347.1 45.0 %all-gather.5.cloned.1.call-start = ((), (), s32[]{:S(2)}) async-start(), calls=%async_computation.16 | async-start | bytes 2621440 | tf_op jit(solution)/shard_map/all_gather | solution.py:210
  372.4 24.7 %all-to-all-start.11 = ((bf16[64,4,1,2]{1,3,2,0:T(2,128)(2,1)}), bf16[64,4,1,2]{1,3,2,0:T(2,128)(2,1)S(1)}, u32[]{:S(2)}, u32[]{:S(2)}) async-start(bf16[64,4,1,2]{1,3,2,0:T(2,128)(2,1)} %constant_dynamic-update-slice_fusion), calls=%async_computation.13 | async-start | bytes 65536 | tf_op jit(solution)/shard_map/all_to_all | solution.py:161
  379.2 12.9 %copy-start.13 = (bf16[128,2048]{1,0:T(8,128)(2,1)S(1)}, bf16[128,2048]{1,0:T(8,128)(2,1)}, u32[]{:S(2)}) copy-start(bf16[128,2048]{1,0:T(8,128)(2,1)} %param.20) | copy-start | bytes 1572868
  383.9 10.5 %copy-start.6 = (f32[512,128]{1,0:T(8,128)S(1)}, f32[512,128]{1,0:T(8,128)}, u32[]{:S(2)}) copy-start(f32[512,128]{1,0:T(8,128)} %copy-done.5) | copy-start | bytes 786436
  383.9 10.5 %copy-start.14 = (bf16[2048,128]{1,0:T(8,128)(2,1)S(1)}, bf16[2048,128]{1,0:T(8,128)(2,1)}, u32[]{:S(2)}) copy-start(bf16[2048,128]{1,0:T(8,128)(2,1)} %param.18) | copy-start | bytes 1572868
  397.1 11.1 %copy-start.8 = (bf16[2048,128]{1,0:T(8,128)(2,1)S(1)}, bf16[2048,128]{1,0:T(8,128)(2,1)}, u32[]{:S(2)}) copy-start(bf16[2048,128]{1,0:T(8,128)(2,1)} %param.19) | copy-start | bytes 1572868
  397.1 62.2 %all-to-all-start.9 = ((bf16[4,64,2,2048]{3,0,2,1:T(4,128)(2,1)}), bf16[4,64,2,2048]{3,0,2,1:T(4,128)(2,1)}, u32[]{:S(2)}, u32[]{:S(2)}) async-start(bf16[4,64,2,2048]{3,0,2,1:T(4,128)(2,1)} %copy.601), calls=%async_computation.11 | async-start | bytes 4194304 | tf_op jit(solution)/shard_map/all_to_all | solution.py:147
  408.2 66.9 %reduce-scatter.5.cloned.1.call-start = ((), (), s32[]{:S(2)}) async-start(), calls=%async_computation.17 | async-start | bytes 2621440 | tf_op jit(solution)/shard_map/reduce_scatter | solution.py:218
  468.6 8.5 %copy-start.1 = (bf16[1,512,2048]{2,1,0:T(8,128)(2,1)S(1)}, bf16[1,512,2048]{2,1,0:T(8,128)(2,1)}, u32[]{:S(2)}) copy-start(bf16[1,512,2048]{2,1,0:T(8,128)(2,1)} %param.17) | copy-start | bytes 6291460
  (10 other events, 24.6 us)
Sparse Core Ops, SparseCore 0:
  121.4 32.5 all-gather.2
  182.3 31.4 reduce-scatter.2
  362.1 29.9 all-gather.4
  412.6 31.9 reduce-scatter.4
